TPU v7x, 32 devices: a whole 2x2x4 slice. The times are simulated.
32 devices in a mesh: row: 4 (over x, core), col: 8 (over z, y).
Axes of the slice: x: 2, y: 2, z: 4, core: 2. Of those that a mesh axis runs over, the one named last changes fastest.
Arguments:
- homolog_embedding: bfloat16 [128, 32, 64], P(None, ('row', 'col')), may hold values from -6 to 6
- standardize_factor: float32 [64], replicated, may hold values from 0.5 to 1.5
- standardize_shift: float32 [64], replicated, may hold values from -3 to 3
- mapping_matrix: bfloat16 [64, 64], replicated, may hold values from -0.75 to 0.75
- output_weight: bfloat16 [1024, 128], replicated, may hold values from -0.1875 to 0.1875
- output_bias: float32 [128], replicated, may hold values from -3 to 3
- cotangent: bfloat16 [32, 32, 128], P('row', 'col'), may hold values from -0.59765625 to 0.59765625
Outputs:
- pair_update_output: bfloat16 [32, 32, 128], P('row', 'col')
- alignment_gradient: float32 [128, 32, 64], P(None, ('row', 'col'))
- projection_gradient: float32 [64, 64], replicated
- output_weight_gradient: float32 [1024, 128], replicated
- norm_gain_gradient: float32 [64], replicated
- norm_bias_gradient: float32 [64], replicated
All inputs are finite; a program needn't handle non-finite values.
Results may differ from a plain program's by a relative error of at most 0.0075.
Values may be sent and summed in bfloat16 or wider, within the bound.
A program may use at most 64 MiB of HBM per device.

v0:
```python
import jax
import jax.numpy as jnp
from jax import lax
from jax.sharding import PartitionSpec as P


def normalized_rows(values, standardize_factor, standardize_shift):
    values = values.astype(jnp.float32)
    mean_row = jnp.mean(values, axis=-1, keepdims=True)
    centred = values - mean_row
    variance = jnp.mean(centred * centred, axis=-1, keepdims=True)
    reciprocal_scale = lax.rsqrt(variance + 1e-05)
    single_unit_rows = centred * reciprocal_scale
    return (
        single_unit_rows * standardize_factor + standardize_shift,
        single_unit_rows,
        reciprocal_scale,
    )


def shards(
    homolog_embedding,
    standardize_factor,
    standardize_shift,
    mapping_matrix,
    output_weight,
    output_bias,
    cotangent,
):
    projection_width = mapping_matrix.shape[1] // 2
    alignment_count = homolog_embedding.shape[0]
    reciprocal_deviation = 1.0 / alignment_count
    block_row_count = cotangent.shape[0]
    block_columns = cotangent.shape[1]
    normalized_complete, single_unit_rows, reciprocal_scale = normalized_rows(
        homolog_embedding, standardize_factor, standardize_shift
    )
    normed = normalized_complete.astype(jnp.bfloat16)
    proj = jnp.einsum(
        "snm,mk->snk", normed, mapping_matrix, preferred_element_type=jnp.float32
    ).astype(jnp.bfloat16)
    row_band = lax.all_gather(proj, "col", axis=1, tiled=True)
    left_band = row_band[..., :projection_width]
    col_index = lax.axis_index("col")
    row_index = lax.axis_index("row")
    row_count = lax.axis_size("row")
    col_count = lax.axis_size("col")
    col_ratio = col_count // row_count
    offset = col_index % col_ratio * block_columns
    gathered = lax.all_gather(proj[..., projection_width:], ("row", "col"), axis=1, tiled=True)
    latter_vertical_band = lax.dynamic_slice_in_dim(
        gathered, col_index * block_columns, block_columns, 1
    )
    block_rows = 1
    for divisor in range(1, block_row_count + 1):
        if block_row_count % divisor == 0 and divisor * block_columns <= 1024:
            block_rows = divisor
    block_count = block_row_count // block_rows

    def one_block(carry, block_index):
        weight_acc, latter_running_total, left_acc = carry
        grad_blk = cotangent.reshape(block_rows * block_columns, -1)
        tensor_product_tile = (
            jnp.einsum(
                "ejt,ecd->jctd", left_band, latter_vertical_band, preferred_element_type=jnp.float32
            )
            * reciprocal_deviation
        )
        tensor_product_tile = tensor_product_tile.astype(jnp.bfloat16).reshape(
            block_rows * block_columns, projection_width * projection_width
        )
        pair_blk = (
            jnp.dot(tensor_product_tile, output_weight, preferred_element_type=jnp.float32)
            + output_bias
        ).astype(jnp.bfloat16)
        grad_outer = lax.dot_general(
            grad_blk, output_weight, (((1,), (1,)), ((), ())), preferred_element_type=jnp.float32
        ).astype(jnp.bfloat16)
        weight_acc = weight_acc + lax.dot_general(
            tensor_product_tile,
            grad_blk,
            (((0,), (0,)), ((), ())),
            preferred_element_type=jnp.float32,
        )
        quadruple_cotangent = grad_outer.reshape(
            block_rows, block_columns, projection_width, projection_width
        )
        former_factor_cotangent = (
            jnp.einsum(
                "lcaz,ycz->yla",
                quadruple_cotangent,
                latter_vertical_band,
                preferred_element_type=jnp.float32,
            )
            * reciprocal_deviation
        )
        latter_running_total = (
            latter_running_total
            + jnp.einsum(
                "wqcp,nwc->nqp", quadruple_cotangent, left_band, preferred_element_type=jnp.float32
            )
            * reciprocal_deviation
        )
        left_acc = former_factor_cotangent
        return (
            (weight_acc, latter_running_total, left_acc),
            pair_blk.reshape(block_rows, block_columns, -1),
        )

    starting_state = (
        jnp.zeros((projection_width * projection_width, output_weight.shape[1]), jnp.float32),
        jnp.zeros((alignment_count, block_columns, projection_width), jnp.float32),
        jnp.zeros((alignment_count, block_row_count, projection_width), jnp.float32),
    )
    (weight_part, right_part, left_part), pair_blocks = lax.scan(
        one_block, starting_state, jnp.arange(block_count, dtype=jnp.int32)
    )
    pair_update_output = pair_blocks.reshape(block_row_count, block_columns, -1)
    right_total = lax.psum(right_part, "row")
    positioned_blocks = jnp.zeros((alignment_count, block_row_count, projection_width), jnp.float32)
    positioned_blocks = lax.dynamic_update_slice_in_dim(positioned_blocks, right_total, offset, 1)
    is_owner = col_index // col_ratio == row_index
    positioned_blocks = jnp.where(is_owner, positioned_blocks, jnp.zeros_like(positioned_blocks))
    returned = jnp.concatenate([left_part, positioned_blocks], axis=-1)
    grad_act = lax.psum_scatter(returned, "col", scatter_dimension=1, tiled=True).astype(
        jnp.bfloat16
    )
    proj_part = jnp.einsum("snm,snk->mk", normed, grad_act, preferred_element_type=jnp.float32)
    grad_normed = jnp.einsum(
        "snk,mk->snm", grad_act, mapping_matrix, preferred_element_type=jnp.float32
    )
    gain_part = jnp.sum(grad_normed * single_unit_rows, axis=(0, 1))
    bias_part = jnp.sum(grad_normed, axis=(0, 1))
    rescaled_values = grad_normed * standardize_factor
    alignment_gradient = reciprocal_scale * (
        rescaled_values
        - jnp.mean(rescaled_values, axis=-1, keepdims=True)
        - single_unit_rows * jnp.mean(rescaled_values * single_unit_rows, axis=-1, keepdims=True)
    )
    output_weight_gradient, projection_gradient, norm_gain_gradient, norm_bias_gradient = lax.psum(
        (weight_part, proj_part, gain_part, bias_part), ("row", "col")
    )
    return (
        pair_update_output,
        alignment_gradient,
        projection_gradient,
        output_weight_gradient,
        norm_gain_gradient,
        norm_bias_gradient,
    )


def solution(mesh):
    in_specs = (P(None, ("row", "col"), None), P(), P(), P(), P(), P(), P("row", "col", None))
    out_specs = (P("row", "col", None), P(None, ("row", "col"), None), P(), P(), P(), P())
    return jax.shard_map(shards, mesh=mesh, in_specs=in_specs, out_specs=out_specs, check_vma=False)
```

profile of v0, /device:TPU:0, one launch (start us, length us, event | category | flops | bytes accessed | tf_op | source)
XLA Modules:
  0.0 253.3 jit_solution(3939034542715303522)
XLA Ops:
  8.0 0.0 all-reduce.4.cloned.1.call-start
  8.1 0.8 convert_reduce_fusion
  8.9 0.6 copy-done.6
  9.6 0.2 convolution_convert_fusion.1
  9.8 32.4 %all-gather = bf16[128,512]{0,1:T(8,128)(2,1)S(1)} all-gather(bf16[128,64]{0,1:T(8,128)(2,1)S(1)} %convolution_convert_fusion.1), channel_id=2, replica_groups=mesh['row'=4,'col'=8] {'col'}, dimensions={1}, use_global_device_ids=true | all-gather | bytes 147456 | tf_op jit(solution)/shard_map/all_gather | solution.py:42
  42.2 0.2 convolution_convert_fusion
  42.4 0.2 reshape.95
  42.6 0.9 fusion.3
  43.5 0.0 all-reduce.4.cloned.1.call-update
  43.5 0.0 reduce-scatter.2.cloned.1.call-start
  43.6 66.2 %all_gather.6 = bf16[128,32,32]{0,2,1:T(8,128)(2,1)S(1)} all-gather(bf16[128,1,32]{0,2,1:T(8,128)(2,1)S(1)} %slice.8), channel_id=1, replica_groups=mesh['row'=4,'col'=8] {'row','col'}, dimensions={1}, use_global_device_ids=true | all-gather | bytes 270336 | tf_op jit(solution)/shard_map/all_gather | solution.py:50
  109.8 0.2 fusion.2
  110.1 0.0 all-reduce.4.cloned.1.call-done
  110.1 0.8 copy-done.2
  110.9 0.7 pad_maximum_fusion
  111.7 0.0 all-reduce.6.cloned.1.call-start
  111.7 0.3 fusion.1
  112.0 0.2 copy.16
  112.2 0.3 reshape.92
  112.5 1.1 fusion.38
  113.5 0.0 all-reduce.6.cloned.1.call-update
  113.5 0.6 copy-done.7
  114.2 0.8 fusion.4
  114.9 55.7 %reduce-scatter.2.cloned.1.call-done = f32[128,1,64]{0,2,1:T(8,128)} async-done(((f32[128,8,64]{0,2,1:T(8,128)}), f32[128,1,64]{0,2,1:T(8,128)}) %reduce-scatter.2.cloned.1.call-update) | async-done | bytes 32784 | tf_op jit(solution)/shard_map/reduce_scatter | solution.py:125
  170.7 1.0 fusion.20
  171.7 0.1 fusion.37
  171.8 0.6 copy-done.3
  172.5 0.2 fusion.27
  172.7 40.9 %all-reduce = (f32[64,64]{1,0:T(8,128)}, f32[64]{0:T(128)}, f32[64]{0:T(128)}) all-reduce(f32[64,64]{1,0:T(8,128)S(1)} %fusion.27, f32[64]{0:T(128)S(1)} %get-tuple-element.25, f32[64]{0:T(128)S(1)} %get-tuple-element.27), channel_id=1, replica_groups=mesh['row'=4,'col'=8] {'row','col'}, use_global_device_ids=true, to_apply=%region_6.7 | all-reduce | flops 4224 | bytes 33792 | tf_op jit(solution)/shard_map/psum | solution.py:140
  213.6 0.7 fusion.19
  214.3 29.8 %all-reduce.6.cloned.1.call-done = f32[1024,128]{1,0:T(8,128)} async-done(((f32[1024,128]{1,0:T(8,128)}), f32[1024,128]{1,0:T(8,128)}) %all-reduce.6.cloned.1.call-update) | async-done | bytes 524304 | tf_op jit(solution)/shard_map/psum | solution.py:140
  244.0 1.9 copy.26
  (22 shorter events, 0.1 us)
Async XLA Ops:
  8.0 34.2 %copy-start = (bf16[1024,128]{1,0:T(8,128)(2,1)S(1)}, bf16[1024,128]{1,0:T(8,128)(2,1)}, u32[]{:S(2)}) copy-start(bf16[1024,128]{1,0:T(8,128)(2,1)} %param.11) | copy-start | bytes 786436
  8.0 0.9 copy-start.1
  8.0 0.9 copy-start.5
  8.0 102.1 %all-reduce.4.cloned.1.call-start = ((), (), s32[]{:S(2)}) async-start(), calls=%async_computation.1 | async-start | bytes 131072 | tf_op jit(solution)/shard_map/psum | solution.py:119
  8.9 0.7 copy-start.6
  8.9 0.7 copy-start.8
  9.8 32.5 %copy-start.4 = (bf16[8,4,128]{2,1,0:T(4,128)(2,1)S(1)}, bf16[8,4,128]{2,1,0:T(4,128)(2,1)}, u32[]{:S(2)}) copy-start(bf16[8,4,128]{2,1,0:T(4,128)(2,1)} %param.13) | copy-start | bytes 24580
  43.5 127.2 %reduce-scatter.2.cloned.1.call-start = ((), (), s32[]{:S(2)}) async-start(), calls=%async_computation.2 | async-start | bytes 294912 | tf_op jit(solution)/shard_map/reduce_scatter | solution.py:125
  110.1 0.8 copy-start.2
  111.7 132.3 %all-reduce.6.cloned.1.call-start = ((), (), s32[]{:S(2)}) async-start(), calls=%async_computation.3 | async-start | bytes 1048576 | tf_op jit(solution)/shard_map/psum | solution.py:140
  113.5 0.7 copy-start.7
  171.7 0.8 copy-start.3
Sparse Core Ops, SparseCore 0:
  43.6 31.9 all-reduce.3
  111.8 58.8 reduce-scatter.1
Sparse Core Ops, SparseCore 1:
  118.9 125.1 all-reduce.5
where the time goes:
time: 254 us; the launch traced here: 253 us
  blocking collectives  140 us (55%)
  waiting for transfers between devices  85.6 us (34%)
  between operations  15.7 us (6%)
  local copies, waits for them, and re-layouts  5.27 us (2%)
  matrix products  4.79 us (2%)
    all_gather x1, blocking collectives, shards(): lax.all_gather(proj[..., projection_width:], ('row', 'col'), axis=1, tile...  66.2 us
    reduce_scatter x1, waiting for transfers between devices, shards(): lax.psum_scatter(returned, 'col', scatter_dimension=1, tiled=True)  55.7 us
    psum x1, blocking collectives, shards(): lax.psum((weight_part, proj_part, gain_part, bias_part), ('row', 'col'))  40.9 us
    all_gather x1, blocking collectives, shards(): row_band = lax.all_gather(proj, 'col', axis=1, tiled=True)  32.4 us
    psum x1, waiting for transfers between devices, shards(): lax.psum((weight_part, proj_part, gain_part, bias_part), ('row', 'col'))  29.8 us
  transfers between devices with their start and end apart: 3, of which 2 were waited for; matrix products, arithmetic and copies ran while one was open for 2% of the time, Pallas kernels for 0%

commit v1 on v0

v1 whole, which is shorter than its diff:
```python
import functools

import jax
import jax.numpy as jnp
from jax import lax
from jax.experimental import pallas as pl
from jax.experimental.pallas import tpu as pltpu
from jax.sharding import PartitionSpec as P

F32, BF16 = jnp.float32, jnp.bfloat16
MESH = pl.DeviceIdType.MESH


def swap_blocks(parts, width):
    axis = parts[0].ndim - 1
    lane = lax.broadcasted_iota(jnp.int32, parts[0].shape, axis)
    a0, a1, a2, a3 = parts
    total = 4 * width
    half = lane < 2 * width
    t0 = jnp.where(half, a0, pltpu.roll(a2, 2 * width, axis))
    t2 = jnp.where(half, pltpu.roll(a0, 2 * width, axis), a2)
    t1 = jnp.where(half, a1, pltpu.roll(a3, 2 * width, axis))
    t3 = jnp.where(half, pltpu.roll(a1, 2 * width, axis), a3)
    even = lane % (2 * width) < width
    u0 = jnp.where(even, t0, pltpu.roll(t1, width, axis))
    u1 = jnp.where(even, pltpu.roll(t0, total - width, axis), t1)
    u2 = jnp.where(even, t2, pltpu.roll(t3, width, axis))
    u3 = jnp.where(even, pltpu.roll(t2, total - width, axis), t3)
    return [u0, u1, u2, u3]


def dot(a, b, ca, cb):
    return lax.dot_general(a, b, (((ca,), (cb,)), ((), ())), preferred_element_type=F32)


def kernel(
    cfg, x_ref, gain_ref, shift_ref, map_ref, w_ref, bias_ref, cot_ref,
    pair_ref, align_ref, proj_ref, wg_ref, gg_ref, bg_ref,
    xbuf, lf, cotf, pairf, glf, sl, sr, rl, rr, s1, r1, s2, r2, gbuf, ebuf,
    x_send, x_recv, e_send, e_recv, s1_send, s1_recv, s2_send, s2_recv,
    g2_send, g2_recv, g1_send, g1_recv,
):
    R, C, BR, BC, S, M, K, CH1, EX, CH2, NO = cfg
    r, c = lax.axis_index("row"), lax.axis_index("col")
    n = r * C + c
    dest_col, dest_slot = lax.div(n, BC), lax.rem(n, BC)
    self_right = dest_col == c
    inv = 1.0 / S

    def other(rr_, cc_):
        return jnp.logical_or(rr_ != r, cc_ != c)

    owners = []
    for k in range(BC):
        o = c * BC + k
        owners.append((lax.div(o, C), lax.rem(o, C)))

    def signal(dev):
        pl.semaphore_signal(barrier, inc=1, device_id=dev, device_id_type=MESH)

    def remote(src, dst, send, recv, dev):
        return pltpu.make_async_remote_copy(
            src_ref=src, dst_ref=dst, send_sem=send, recv_sem=recv, device_id=dev, device_id_type=MESH
        )

    barrier = pltpu.get_barrier_semaphore()
    for off in range(1, C):
        signal((r, lax.rem(c + off, C)))
    for off in range(1, R):
        signal((lax.rem(r + off, R), c))
    for q in range(R):
        @pl.when(other(q, dest_col))
        def _():
            signal((q, dest_col))
    for k in range(BC):
        @pl.when(other(*owners[k]))
        def _():
            signal(owners[k])

    own = jnp.transpose(x_ref[...].astype(F32))
    own16 = own.astype(BF16)
    xbuf[c] = own16

    @pl.when(self_right)
    def _():
        xbuf[BR + dest_slot] = own16

    pl.semaphore_wait(barrier, C - 1 + R - 1 + R + BC - jnp.where(self_right, 2, 0))

    pending = []
    for q in range(R):
        cp = remote(
            xbuf.at[c], xbuf.at[BR + dest_slot], x_send.at[C + q], x_recv.at[BR + dest_slot], (q, dest_col)
        )
        cond = other(q, dest_col)

        @pl.when(cond)
        def _():
            cp.start()
        pending.append((cp, cond))
    for off in range(1, C):
        q = lax.rem(c + off, C)
        cp = remote(xbuf.at[c], xbuf.at[c], x_send.at[q], x_recv.at[c], (r, q))
        cp.start()
        pending.append((cp, None))

    factor = jnp.transpose(jnp.broadcast_to(gain_ref[...], (S, M)))
    shift = jnp.transpose(jnp.broadcast_to(shift_ref[...], (S, M)))
    mapping = map_ref[...]
    mapping_t = jnp.transpose(mapping.astype(F32)).astype(BF16)
    cotf[...] = cot_ref[...].astype(F32)
    cot = jnp.concatenate([cotf[pl.ds(j, BR, stride=BC), :] for j in range(BC)], axis=0).astype(BF16)
    w = w_ref[...]
    groups = K * K // 128
    G = dot(cot, w, 1, 1).astype(BF16).astype(F32)
    tiles = []
    for t in range(BC // 4):
        parts = []
        for j in range(4):
            row = (4 * t + j) * BR
            parts.append(jnp.stack([G[row:row + BR, 128 * g:128 * g + 128] for g in range(groups)], axis=0))
        b = swap_blocks(parts, K)
        tiles.append(jnp.stack(b, axis=1).reshape(K * BR, 128))
    g2 = jnp.concatenate(tiles, axis=1).astype(BF16)

    def standardized(x):
        mean = jnp.mean(x, axis=0, keepdims=True)
        cen = x - mean
        scale = lax.rsqrt(jnp.mean(cen * cen, axis=0, keepdims=True) + 1e-05)
        return cen * scale, scale

    own_unit, own_scale = standardized(own)

    for off in range(1, C):
        q = lax.rem(c + off, C)
        remote(xbuf.at[q], xbuf.at[q], x_send.at[q], x_recv.at[q], (r, q)).wait_recv()
    for k in range(BC):
        @pl.when(other(*owners[k]))
        def _():
            remote(
                xbuf.at[BR + k], xbuf.at[BR + k], x_send.at[0], x_recv.at[BR + k], owners[k]
            ).wait_recv()

    units, normeds = [], []
    for i in range(BR + BC):
        unit, _ = standardized(xbuf[i].astype(F32))
        units.append(unit)
        normeds.append((unit * factor + shift).astype(BF16))
    normed = jnp.concatenate(normeds, axis=1)
    proj = dot(mapping_t, normed, 1, 0)
    for i in range(BR):
        lf[pl.ds(i, K, stride=BR), :] = proj[:K, S * i:S * i + S].astype(BF16).astype(F32)
    left = lf[...].astype(BF16)
    right = jnp.concatenate(
        [proj[K:, S * (BR + j):S * (BR + j) + S] for j in range(BC)], axis=0
    ).astype(BF16)
    outer = (dot(left, right, 1, 1) * inv).astype(BF16).astype(F32)
    rows = []
    for t in range(BC // 4):
        o = outer[:, 128 * t:128 * t + 128].reshape(groups, 4, BR, 128)
        b = swap_blocks([o[:, q] for q in range(4)], K)
        for j in range(4):
            rows.append(jnp.concatenate([b[j][g] for g in range(groups)], axis=1))
    ot = jnp.concatenate(rows, axis=0).astype(BF16)

    wgrad = dot(ot, cot, 0, 0).astype(BF16)
    for p in range(R):
        s1[p, :CH1, :] = wgrad[p * CH1:(p + 1) * CH1]

    glf[...] = dot(g2, right, 1, 0) * inv
    gr = (dot(g2, left, 0, 0) * inv).astype(BF16)
    gls = []
    for i in range(BR):
        gl = glf[pl.ds(i, K, stride=BR), :].astype(BF16)
        gls.append(gl)
        sl[i] = gl
    grs = []
    for j in range(BC):
        gg = gr[j * K:(j + 1) * K]
        grs.append(gg)
        sr[j] = gg
    rl[c] = sl[c]

    @pl.when(self_right)
    def _():
        rr[r] = sr[dest_slot]

    for off in range(1, C):
        q = lax.rem(c + off, C)
        cp = remote(sl.at[q], rl.at[c], e_send.at[q], e_recv.at[c], (r, q))
        cp.start()
        pending.append((cp, None))
    for k in range(BC):
        cp = remote(sr.at[k], rr.at[r], e_send.at[C + k], e_recv.at[C + r], owners[k])
        cond = other(*owners[k])

        @pl.when(cond)
        def _():
            cp.start()
        pending.append((cp, cond))

    glc = jnp.concatenate(gls, axis=1)
    grc = jnp.concatenate(grs, axis=1)
    cut = BR * S
    ebuf[...] = jnp.zeros_like(ebuf)
    ebuf[:, :K] = dot(normed[:, :cut], glc, 1, 1)
    ebuf[:, K:2 * K] = dot(normed[:, cut:], grc, 1, 1)
    gn = jnp.concatenate([dot(mapping[:, :K], glc, 1, 0), dot(mapping[:, K:], grc, 1, 0)], axis=1)
    bsum, gsum = jnp.zeros((M, S), F32), jnp.zeros((M, S), F32)
    for i in range(BR + BC):
        piece = gn[:, S * i:S * i + S]
        bsum = bsum + piece
        gsum = gsum + piece * units[i]
    ebuf[:, 2 * K:2 * K + 1] = jnp.sum(gsum, axis=1, keepdims=True)
    ebuf[:, 2 * K + 1:2 * K + 2] = jnp.sum(bsum, axis=1, keepdims=True)
    extra = ebuf[...].astype(BF16)
    for p in range(R):
        if p * EX < M:
            s1[p, CH1:, :] = extra[p * EX:(p + 1) * EX]
        else:
            s1[p, CH1:, :] = jnp.zeros((EX, 128), BF16)

    for off in range(1, R):
        p = lax.rem(r + off, R)
        cp = remote(s1.at[p], r1.at[r], s1_send.at[p], s1_recv.at[r], (p, c))
        cp.start()
        pending.append((cp, None))
    r1[r] = s1[r]
    for off in range(1, R):
        p = lax.rem(r + off, R)
        remote(s1.at[p], r1.at[p], s1_send.at[p], s1_recv.at[p], (p, c)).wait_recv()
    acc = r1[0].astype(F32)
    for p in range(1, R):
        acc = acc + r1[p].astype(F32)
    acc = acc.astype(BF16)
    for q in range(C):
        u = q % NO
        s2[q, :CH2, :] = acc[u * CH2:(u + 1) * CH2]
        s2[q, CH2:, :] = acc[CH1:]

    for off in range(1, C):
        q = lax.rem(c + off, C)
        cp = remote(s2.at[q], r2.at[c], s2_send.at[q], s2_recv.at[c], (r, q))
        cp.start()
        pending.append((cp, None))
    r2[c] = s2[c]

    for off in range(1, C):
        q = lax.rem(c + off, C)
        remote(sl.at[q], rl.at[q], e_send.at[q], e_recv.at[q], (r, q)).wait_recv()
    for q in range(R):
        @pl.when(other(q, dest_col))
        def _():
            remote(sr.at[0], rr.at[q], e_send.at[C], e_recv.at[C + q], (q, dest_col)).wait_recv()
    al = rl[0].astype(F32)
    for q in range(1, C):
        al = al + rl[q].astype(F32)
    ar = rr[0].astype(F32)
    for q in range(1, R):
        ar = ar + rr[q].astype(F32)
    act = jnp.concatenate([al, ar], axis=0).astype(BF16)
    scaled = dot(mapping, act, 1, 0) * factor
    align = own_scale * (
        scaled
        - jnp.mean(scaled, axis=0, keepdims=True)
        - own_unit * jnp.mean(scaled * own_unit, axis=0, keepdims=True)
    )
    align_ref[...] = jnp.transpose(align)
    pairs = dot(ot, w, 1, 0) + bias_ref[...]
    for j in range(BC):
        pairf[pl.ds(j, BR, stride=BC), :] = pairs[j * BR:(j + 1) * BR]
    pair_ref[...] = pairf[...].astype(BF16)

    for off in range(1, C):
        q = lax.rem(c + off, C)
        remote(s2.at[q], r2.at[q], s2_send.at[q], s2_recv.at[q], (r, q)).wait_recv()
    acc = r2[0].astype(F32)
    for q in range(1, C):
        acc = acc + r2[q].astype(F32)
    acc = acc.astype(BF16)
    gbuf[r, CH1:, :] = acc[CH2:]

    place = pl.ds(pl.multiple_of(lax.rem(c, NO) * CH2, 16), CH2)

    def spread():
        gbuf[r, place, :] = acc[:CH2]
        for off in range(1, C):
            q = lax.rem(c + off, C)
            remote(gbuf.at[r, place], gbuf.at[r, place], g2_send.at[q], g2_recv.at[c], (r, q)).start()

    def spread_done():
        for off in range(1, C):
            q = lax.rem(c + off, C)
            remote(gbuf.at[r, place], gbuf.at[r, place], g2_send.at[q], g2_recv.at[c], (r, q)).wait_send()

    if NO == C:
        spread()
    else:
        pl.when(c < NO)(spread)
    for q in range(NO):
        where = pl.ds(q * CH2, CH2)

        @pl.when(c != q)
        def _():
            remote(gbuf.at[r, where], gbuf.at[r, where], g2_send.at[q], g2_recv.at[q], (r, q)).wait_recv()
    for off in range(1, R):
        p = lax.rem(r + off, R)
        cp = remote(gbuf.at[r], gbuf.at[r], g1_send.at[p], g1_recv.at[r], (p, c))
        cp.start()
        pending.append((cp, None))
    for off in range(1, R):
        p = lax.rem(r + off, R)
        remote(gbuf.at[p], gbuf.at[p], g1_send.at[p], g1_recv.at[p], (p, c)).wait_recv()
    for p in range(R):
        wg_ref[p * CH1:(p + 1) * CH1, :] = gbuf[p, :CH1, :].astype(F32)
        if p * EX < M:
            ebuf[p * EX:(p + 1) * EX, :] = gbuf[p, CH1:, :].astype(F32)
    proj_ref[...] = ebuf[:, :2 * K]
    flipped = jnp.transpose(ebuf[...])
    gg_ref[...] = flipped[2 * K:2 * K + 1, :]
    bg_ref[...] = flipped[2 * K + 1:2 * K + 2, :]

    if NO == C:
        spread_done()
    else:
        pl.when(c < NO)(spread_done)
    for cp, cond in pending:
        if cond is None:
            cp.wait_send()
        else:
            pl.when(cond)(cp.wait_send)


def shards(x, gain, shift, mapping, w, bias, cot):
    R, C = lax.axis_size("row"), lax.axis_size("col")
    S, M = x.shape[0], x.shape[2]
    K = mapping.shape[1] // 2
    BR, BC, E = cot.shape
    rows = w.shape[0]
    CH1, EX = rows // R, max(16, M // R)
    CH2 = max(16, CH1 // C)
    NO = CH1 // CH2
    cfg = (R, C, BR, BC, S, M, K, CH1, EX, CH2, NO)
    vm = pl.BlockSpec(memory_space=pltpu.VMEM)
    sem = pltpu.SemaphoreType.DMA
    pair, align, proj, wg, gg, bg = pl.pallas_call(
        functools.partial(kernel, cfg),
        out_shape=[
            jax.ShapeDtypeStruct((BR * BC, E), BF16),
            jax.ShapeDtypeStruct((S, M), F32),
            jax.ShapeDtypeStruct((M, 2 * K), F32),
            jax.ShapeDtypeStruct((rows, E), F32),
            jax.ShapeDtypeStruct((1, M), F32),
            jax.ShapeDtypeStruct((1, M), F32),
        ],
        in_specs=[vm] * 7,
        out_specs=[vm] * 6,
        scratch_shapes=[
            pltpu.VMEM((BR + BC, M, S), BF16),
            pltpu.VMEM((K * BR, S), F32),
            pltpu.VMEM((BR * BC, E), F32),
            pltpu.VMEM((BR * BC, E), F32),
            pltpu.VMEM((K * BR, S), F32),
            pltpu.VMEM((BR, K, S), BF16),
            pltpu.VMEM((BC, K, S), BF16),
            pltpu.VMEM((C, K, S), BF16),
            pltpu.VMEM((R, K, S), BF16),
            pltpu.VMEM((R, CH1 + EX, E), BF16),
            pltpu.VMEM((R, CH1 + EX, E), BF16),
            pltpu.VMEM((C, CH2 + EX, E), BF16),
            pltpu.VMEM((C, CH2 + EX, E), BF16),
            pltpu.VMEM((R, CH1 + EX, E), BF16),
            pltpu.VMEM((M, E), F32),
            sem((C + R,)), sem((BR + BC,)),
            sem((C + BC,)), sem((C + R,)),
            sem((R,)), sem((R,)),
            sem((C,)), sem((C,)),
            sem((C,)), sem((C,)),
            sem((R,)), sem((R,)),
        ],
        compiler_params=pltpu.CompilerParams(
            collective_id=0, has_side_effects=True, vmem_limit_bytes=48 * 1024 * 1024
        ),
        name="outer_mean",
    )(
        x.reshape(S, M), gain.reshape(1, M), shift.reshape(1, M), mapping, w,
        bias.reshape(1, E), cot.reshape(BR * BC, E),
    )
    return (
        pair.reshape(BR, BC, E), align.reshape(S, 1, M), proj, wg, gg.reshape(M), bg.reshape(M)
    )


def solution(mesh):
    in_specs = (P(None, ("row", "col"), None), P(), P(), P(), P(), P(), P("row", "col", None))
    out_specs = (P("row", "col", None), P(None, ("row", "col"), None), P(), P(), P(), P())
    return jax.shard_map(shards, mesh=mesh, in_specs=in_specs, out_specs=out_specs, check_vma=False)
```

time: 254 us -> 39.9 us (0.16)
  blocking collectives: 140 us -> 0 us
  waiting for transfers between devices: 85.6 us -> 0 us
  Pallas kernels: 0 us -> 32.7 us
  between operations: 15.7 us -> 0.7 us
  matrix products: 4.79 us -> 0 us
    all_gather x2 -> x0, blocking collectives: 98.7 us -> none  [the longest x1 66.2 us: shards(): lax.all_gather(proj[..., projection_width:], ('row', 'col'), axis=1, tile...]
    reduce_scatter x1 -> x0, waiting for transfers between devices: 55.7 us -> none  [shards(): lax.psum_scatter(returned, 'col', scatter_dimension=1, tiled=True)]
    psum x1 -> x0, blocking collectives: 40.9 us -> none  [shards(): lax.psum((weight_part, proj_part, gain_part, bias_part), ('row', 'col'))]
    pallas_call x0 -> x1, Pallas kernels: none -> 32.7 us  [shards(): pl.pallas_call(functools.partial(kernel, cfg), out_shape=[jax.ShapeDtypeS...]
    psum x2 -> x0, waiting for transfers between devices: 29.8 us -> none  [the longest x1 29.8 us: shards(): lax.psum((weight_part, proj_part, gain_part, bias_part), ('row', 'col'))]
    dot_general x9 -> x0, matrix products: 4.79 us -> none  [the longest x1 1.06 us: one_block(): lax.dot_general(tensor_product_tile, grad_blk, (((0,), (0,)), ((), ())),...]
  transfers between devices with their start and end apart: 3 -> 0, of which waited for: 2 -> 0; matrix products, arithmetic and copies ran while one was open for 2% -> 0% of each run, Pallas kernels for 0% -> 0%
where the time goes in v1:
time: 39.9 us; the launch traced here: 39.6 us
  Pallas kernels  32.7 us (82%)
  local copies, waits for them, and re-layouts  6.17 us (15%)
  between operations  0.7 us (2%)
    pallas_call x1, Pallas kernels, shards(): pl.pallas_call(functools.partial(kernel, cfg), out_shape=[jax.ShapeDtypeS...  32.7 us
    unnamed x19, local copies, waits for them, and re-layouts  6.17 us

profile of v1, /device:TPU:0, one launch (start us, length us, event | category | flops | bytes accessed | tf_op | source)
XLA Modules:
  0.0 39.6 jit_solution(13355356593945765110)
XLA Ops:
  0.6 0.0 copy-start.1
  0.6 0.0 copy-start.2
  0.7 0.8 %copy.13 = bf16[128,1,64]{2,0,1:T(8,128)(2,1)S(1)} copy(bf16[128,1,64]{0,2,1:T(8,128)(2,1)} %param.7) | data formatting | bytes 32768 | tf_op args[0]
  1.5 0.0 copy-start.3
  1.5 0.0 copy-start.4
  1.5 0.0 copy-start.5
  1.5 0.0 copy-done.1
  1.5 0.0 copy-done.2
  1.5 0.6 %copy-done.3 = f32[64]{0:T(128)S(1)} copy-done((f32[64]{0:T(128)S(1)}, f32[64]{0:T(128)}, u32[]{:S(2)}) %copy-start.3) | copy-done | bytes 280
  2.2 0.0 copy-done.4
  2.2 0.0 copy-done.5
  2.2 0.0 copy-start
  2.2 0.9 %copy-done = bf16[1024,128]{1,0:T(8,128)(2,1)S(1)} copy-done((bf16[1024,128]{1,0:T(8,128)(2,1)S(1)}, bf16[1024,128]{1,0:T(8,128)(2,1)}, u32[]{:S(2)}) %copy-start) | copy-done | bytes 262168
  3.1 32.7 %outer_mean.1 = (bf16[32,128]{1,0:T(8,128)(2,1)S(1)}, f32[128,64]{1,0:T(8,128)S(1)}, f32[64,64]{1,0:T(8,128)S(1)}, f32[1024,128]{1,0:T(8,128)S(1)}, f32[1,64]{1,0:T(1,128)S(1)}, /*index=5*/f32[1,64]{1,0:T(1,128)S(1)}) custom-call(bf16[128,64]{1,0:T(8,128)(2,1)S(1)} %bitcast.9, f32[1,64]{1,0:T(1,128)S(1)} %bitcast.13, f32[1,64]{1,0:T(1,128)S(1)} %bitcast.14, ...), custom_call_target="tpu_custom_call" | custom-call | tf_op jit(solution)/shard_map/outer_mean/pallas_call | solution.py:346
  35.8 0.7 %copy.14 = f32[128,1,64]{0,2,1:T(8,128)} copy(f32[128,1,64]{2,0,1:T(8,128)S(1)} %bitcast.10) | data formatting | bytes 65536
  36.5 0.6 %copy.20 = bf16[8,4,128]{2,1,0:T(4,128)(2,1)} copy(bf16[8,4,128]{2,1,0:T(4,128)(2,1)S(1)} %bitcast.12) | data formatting | bytes 16384
  37.1 0.6 %copy.21 = f32[64,64]{1,0:T(8,128)} copy(f32[64,64]{1,0:T(8,128)S(1)} %get-tuple-element.32) | data formatting | bytes 32768
  37.8 0.8 %copy.22 = f32[1024,128]{1,0:T(8,128)} copy(f32[1024,128]{1,0:T(8,128)S(1)} %get-tuple-element.33) | data formatting | bytes 1048576
  38.5 0.5 %copy.23 = f32[64]{0:T(128)} copy(f32[64]{0:T(128)S(1)} %bitcast.17) | data formatting | bytes 512
  39.1 0.5 %copy.24 = f32[64]{0:T(128)} copy(f32[64]{0:T(128)S(1)} %bitcast.16) | data formatting | bytes 512
Async XLA Ops:
  0.6 0.9 %copy-start.1 = (bf16[64,64]{1,0:T(8,128)(2,1)S(1)}, bf16[64,64]{1,0:T(8,128)(2,1)}, u32[]{:S(2)}) copy-start(bf16[64,64]{1,0:T(8,128)(2,1)} %map_ref.1) | copy-start | bytes 24580
  0.6 0.9 %copy-start.2 = (bf16[8,4,128]{2,1,0:T(4,128)(2,1)S(1)}, bf16[8,4,128]{2,1,0:T(4,128)(2,1)}, u32[]{:S(2)}) copy-start(bf16[8,4,128]{2,1,0:T(4,128)(2,1)} %param.13) | copy-start | bytes 24580
  1.5 0.7 %copy-start.3 = (f32[64]{0:T(128)S(1)}, f32[64]{0:T(128)}, u32[]{:S(2)}) copy-start(f32[64]{0:T(128)} %param.8) | copy-start | bytes 772
  1.5 0.7 %copy-start.4 = (f32[64]{0:T(128)S(1)}, f32[64]{0:T(128)}, u32[]{:S(2)}) copy-start(f32[64]{0:T(128)} %param.9) | copy-start | bytes 772
  1.5 0.7 %copy-start.5 = (f32[128]{0:T(128)S(1)}, f32[128]{0:T(128)}, u32[]{:S(2)}) copy-start(f32[128]{0:T(128)} %param.12) | copy-start | bytes 1540
  2.2 0.9 %copy-start = (bf16[1024,128]{1,0:T(8,128)(2,1)S(1)}, bf16[1024,128]{1,0:T(8,128)(2,1)}, u32[]{:S(2)}) copy-start(bf16[1024,128]{1,0:T(8,128)(2,1)} %w_ref.1) | copy-start | bytes 786436

commit v2 on v1

v2 whole, which is shorter than its diff:
```python
import functools

import jax
import jax.numpy as jnp
from jax import lax
from jax.experimental import pallas as pl
from jax.experimental.pallas import tpu as pltpu
from jax.sharding import PartitionSpec as P

F32, BF16 = jnp.float32, jnp.bfloat16
MESH = pl.DeviceIdType.MESH


def swap_blocks(parts, width):
    axis = parts[0].ndim - 1
    lane = lax.broadcasted_iota(jnp.int32, parts[0].shape, axis)
    a0, a1, a2, a3 = parts
    total = 4 * width
    half = lane < 2 * width
    t0 = jnp.where(half, a0, pltpu.roll(a2, 2 * width, axis))
    t2 = jnp.where(half, pltpu.roll(a0, 2 * width, axis), a2)
    t1 = jnp.where(half, a1, pltpu.roll(a3, 2 * width, axis))
    t3 = jnp.where(half, pltpu.roll(a1, 2 * width, axis), a3)
    even = lane % (2 * width) < width
    u0 = jnp.where(even, t0, pltpu.roll(t1, width, axis))
    u1 = jnp.where(even, pltpu.roll(t0, total - width, axis), t1)
    u2 = jnp.where(even, t2, pltpu.roll(t3, width, axis))
    u3 = jnp.where(even, pltpu.roll(t2, total - width, axis), t3)
    return [u0, u1, u2, u3]


def dot(a, b, ca, cb):
    return lax.dot_general(a, b, (((ca,), (cb,)), ((), ())), preferred_element_type=F32)


def kernel(
    cfg, x_hbm, gain_hbm, shift_hbm, map_hbm, w_hbm, bias_hbm, cot_hbm,
    pair_ref, align_ref, gout_ref, gxout_ref,
    gain_ref, shift_ref, map_ref, w_ref, bias_ref, cot_ref,
    xbuf, lf, cotf, pairf, glf, sl, sr, rl, rr, s1, r1, s2, r2, gbuf, ebuf, s1x, r1x, r2x, gx,
    load, x_send, x_recv, e_send, e_recv, s1_send, s1_recv, s2_send, s2_recv,
    g2_send, g2_recv, g1_send, g1_recv, x1_send, x1_recv, x2_send, x2_recv, x3_send, x3_recv,
):
    R, C, BR, BC, S, M, K, CH1, EX, CH2, NO = cfg
    r, c = lax.axis_index("row"), lax.axis_index("col")
    n = r * C + c
    dest_col, dest_slot = lax.div(n, BC), lax.rem(n, BC)
    self_right = dest_col == c
    inv = 1.0 / S
    row_peers = [lax.rem(r + off, R) for off in range(1, R)]
    col_peers = [lax.rem(c + off, C) for off in range(1, C)]

    loads = [
        pltpu.make_async_copy(src, dst, load.at[i])
        for i, (src, dst) in enumerate([
            (x_hbm, xbuf.at[c]), (cot_hbm, cot_ref), (w_hbm, w_ref), (map_hbm, map_ref),
            (gain_hbm, gain_ref), (shift_hbm, shift_ref), (bias_hbm, bias_ref),
        ])
    ]
    for cp in loads:
        cp.start()

    def other(rr_, cc_):
        return jnp.logical_or(rr_ != r, cc_ != c)

    owners = []
    for k in range(BC):
        o = c * BC + k
        owners.append((lax.div(o, C), lax.rem(o, C)))

    def signal(dev):
        pl.semaphore_signal(barrier, inc=1, device_id=dev, device_id_type=MESH)

    def remote(src, dst, send, recv, dev):
        return pltpu.make_async_remote_copy(
            src_ref=src, dst_ref=dst, send_sem=send, recv_sem=recv, device_id=dev, device_id_type=MESH
        )

    def owning(q, f):
        if NO == C:
            f()
        else:
            pl.when(q < NO)(f)

    barrier = pltpu.get_barrier_semaphore()
    for q in col_peers:
        signal((r, q))
    for p in row_peers:
        signal((p, c))
    for q in range(R):
        @pl.when(other(q, dest_col))
        def _():
            signal((q, dest_col))
    for k in range(BC):
        @pl.when(other(*owners[k]))
        def _():
            signal(owners[k])

    loads[0].wait()

    @pl.when(self_right)
    def _():
        xbuf[BR + dest_slot] = xbuf[c]

    pl.semaphore_wait(barrier, C - 1 + R - 1 + R + BC - jnp.where(self_right, 2, 0))

    pending = []

    def send(src, dst, ssem, rsem, dev, cond=None):
        cp = remote(src, dst, ssem, rsem, dev)
        if cond is None:
            cp.start()
        else:
            pl.when(cond)(cp.start)
        pending.append((cp, cond))

    for q in range(R):
        send(
            xbuf.at[c], xbuf.at[BR + dest_slot], x_send.at[C + q], x_recv.at[BR + dest_slot],
            (q, dest_col), other(q, dest_col),
        )
    for q in col_peers:
        send(xbuf.at[c], xbuf.at[c], x_send.at[q], x_recv.at[c], (r, q))

    for cp in loads[1:]:
        cp.wait()
    factor = jnp.transpose(jnp.broadcast_to(gain_ref[...], (S, M)))
    shift = jnp.transpose(jnp.broadcast_to(shift_ref[...], (S, M)))
    mapping = map_ref[...]
    mapping_t = jnp.transpose(mapping.astype(F32)).astype(BF16)
    cotf[...] = cot_ref[...].astype(F32)
    cot = jnp.concatenate([cotf[pl.ds(j, BR, stride=BC), :] for j in range(BC)], axis=0).astype(BF16)
    w = w_ref[...]
    groups = K * K // 128
    G = dot(cot, w, 1, 1).astype(BF16).astype(F32)
    tiles = []
    for t in range(BC // 4):
        parts = []
        for j in range(4):
            row = (4 * t + j) * BR
            parts.append(jnp.stack([G[row:row + BR, 128 * g:128 * g + 128] for g in range(groups)], axis=0))
        b = swap_blocks(parts, K)
        tiles.append(jnp.stack(b, axis=1).reshape(K * BR, 128))
    g2 = jnp.concatenate(tiles, axis=1).astype(BF16)

    def standardized(x):
        mean = jnp.mean(x, axis=0, keepdims=True)
        cen = x - mean
        scale = lax.rsqrt(jnp.mean(cen * cen, axis=0, keepdims=True) + 1e-05)
        return cen * scale, scale

    own_unit, own_scale = standardized(xbuf[c].astype(F32))

    for q in col_peers:
        remote(xbuf.at[q], xbuf.at[q], x_send.at[q], x_recv.at[q], (r, q)).wait_recv()
    for k in range(BC):
        @pl.when(other(*owners[k]))
        def _():
            remote(
                xbuf.at[BR + k], xbuf.at[BR + k], x_send.at[0], x_recv.at[BR + k], owners[k]
            ).wait_recv()

    units, normeds = [], []
    for i in range(BR + BC):
        unit, _ = standardized(xbuf[i].astype(F32))
        units.append(unit)
        normeds.append((unit * factor + shift).astype(BF16))
    normed = jnp.concatenate(normeds, axis=1)
    proj = dot(mapping_t, normed, 1, 0)
    for i in range(BR):
        lf[pl.ds(i, K, stride=BR), :] = proj[:K, S * i:S * i + S].astype(BF16).astype(F32)
    left = lf[...].astype(BF16)
    right = jnp.concatenate(
        [proj[K:, S * (BR + j):S * (BR + j) + S] for j in range(BC)], axis=0
    ).astype(BF16)
    outer = (dot(left, right, 1, 1) * inv).astype(BF16).astype(F32)
    rows = []
    for t in range(BC // 4):
        o = outer[:, 128 * t:128 * t + 128].reshape(groups, 4, BR, 128)
        b = swap_blocks([o[:, q] for q in range(4)], K)
        for j in range(4):
            rows.append(jnp.concatenate([b[j][g] for g in range(groups)], axis=1))
    ot = jnp.concatenate(rows, axis=0).astype(BF16)

    wgrad = dot(ot, cot, 0, 0).astype(BF16)
    for p in range(R):
        s1[p] = wgrad[p * CH1:(p + 1) * CH1]
    for p in row_peers:
        send(s1.at[p], r1.at[r], s1_send.at[p], s1_recv.at[r], (p, c))

    glf[...] = dot(g2, right, 1, 0) * inv
    gr = (dot(g2, left, 0, 0) * inv).astype(BF16)
    gls = []
    for i in range(BR):
        gl = glf[pl.ds(i, K, stride=BR), :].astype(BF16)
        gls.append(gl)
        sl[i] = gl
    grs = []
    for j in range(BC):
        gg = gr[j * K:(j + 1) * K]
        grs.append(gg)
        sr[j] = gg
    rl[c] = sl[c]

    @pl.when(self_right)
    def _():
        rr[r] = sr[dest_slot]

    for q in col_peers:
        send(sl.at[q], rl.at[c], e_send.at[q], e_recv.at[c], (r, q))
    for k in range(BC):
        send(sr.at[k], rr.at[r], e_send.at[C + k], e_recv.at[C + r], owners[k], other(*owners[k]))

    glc = jnp.concatenate(gls, axis=1)
    grc = jnp.concatenate(grs, axis=1)
    cut = BR * S
    ebuf[...] = jnp.zeros_like(ebuf)
    ebuf[:, :K] = dot(normed[:, :cut], glc, 1, 1)
    ebuf[:, K:2 * K] = dot(normed[:, cut:], grc, 1, 1)
    gn = jnp.concatenate([dot(mapping[:, :K], glc, 1, 0), dot(mapping[:, K:], grc, 1, 0)], axis=1)
    bsum, gsum = jnp.zeros((M, S), F32), jnp.zeros((M, S), F32)
    for i in range(BR + BC):
        piece = gn[:, S * i:S * i + S]
        bsum = bsum + piece
        gsum = gsum + piece * units[i]
    ebuf[:, 2 * K:2 * K + 1] = jnp.sum(gsum, axis=1, keepdims=True)
    ebuf[:, 2 * K + 1:2 * K + 2] = jnp.sum(bsum, axis=1, keepdims=True)
    extra = ebuf[...].astype(BF16)
    for p in range(R):
        if p * EX < M:
            s1x[p] = extra[p * EX:(p + 1) * EX]
        else:
            s1x[p] = jnp.zeros((EX, 128), BF16)
    for p in row_peers:
        send(s1x.at[p], r1x.at[r], x1_send.at[p], x1_recv.at[r], (p, c))

    def total(buf, count):
        acc = buf[0].astype(F32)
        for p in range(1, count):
            acc = acc + buf[p].astype(F32)
        return acc

    r1[r] = s1[r]
    for p in row_peers:
        remote(s1.at[p], r1.at[p], s1_send.at[p], s1_recv.at[p], (p, c)).wait_recv()
    s2[...] = total(r1, R).astype(BF16)

    def chunk(q):
        return pl.ds(pl.multiple_of(lax.rem(q, NO) * CH2, 16), CH2)

    for q in col_peers:
        send(s2.at[chunk(q)], r2.at[c], s2_send.at[q], s2_recv.at[c], (r, q))
    r2[c] = s2[chunk(c)]

    r1x[r] = s1x[r]
    for p in row_peers:
        remote(s1x.at[p], r1x.at[p], x1_send.at[p], x1_recv.at[p], (p, c)).wait_recv()
    r2x[c] = total(r1x, R).astype(BF16)
    for q in col_peers:
        send(r2x.at[c], r2x.at[c], x2_send.at[q], x2_recv.at[c], (r, q))

    pairs = dot(ot, w, 1, 0) + bias_ref[...]
    for j in range(BC):
        pairf[pl.ds(j, BR, stride=BC), :] = pairs[j * BR:(j + 1) * BR]
    pair_ref[...] = pairf[...].astype(BF16)

    for q in col_peers:
        remote(s2.at[chunk(q)], r2.at[q], s2_send.at[q], s2_recv.at[q], (r, q)).wait_recv()

    mine = chunk(c)
    result = total(r2, C).astype(BF16)

    def forward(q):
        place = chunk(q)
        for p in row_peers:
            remote(
                gbuf.at[r, place], gbuf.at[r, place], g1_send.at[p * NO + q], g1_recv.at[r * NO + q], (p, c)
            ).start()

    def spread():
        gbuf[r, mine, :] = result
        for q in col_peers:
            remote(gbuf.at[r, mine], gbuf.at[r, mine], g2_send.at[q], g2_recv.at[c], (r, q)).start()
        forward(c)

    owning(c, spread)

    for q in col_peers:
        remote(r2x.at[q], r2x.at[q], x2_send.at[q], x2_recv.at[q], (r, q)).wait_recv()
    gx[r] = total(r2x, C).astype(BF16)
    for p in row_peers:
        send(gx.at[r], gx.at[r], x3_send.at[p], x3_recv.at[r], (p, c))

    for q in col_peers:
        remote(sl.at[q], rl.at[q], e_send.at[q], e_recv.at[q], (r, q)).wait_recv()
    for q in range(R):
        @pl.when(other(q, dest_col))
        def _():
            remote(sr.at[0], rr.at[q], e_send.at[C], e_recv.at[C + q], (q, dest_col)).wait_recv()
    act = jnp.concatenate([total(rl, C), total(rr, R)], axis=0).astype(BF16)
    scaled = dot(mapping, act, 1, 0) * factor
    align_ref[...] = own_scale * (
        scaled
        - jnp.mean(scaled, axis=0, keepdims=True)
        - own_unit * jnp.mean(scaled * own_unit, axis=0, keepdims=True)
    )

    for q in col_peers:
        def pass_on():
            place = chunk(q)
            remote(gbuf.at[r, place], gbuf.at[r, place], g2_send.at[q], g2_recv.at[q], (r, q)).wait_recv()
            forward(q)
        owning(q, pass_on)
    for p in row_peers:
        remote(gx.at[p], gx.at[p], x3_send.at[p], x3_recv.at[p], (p, c)).wait_recv()
        for q in range(NO):
            place = pl.ds(q * CH2, CH2)
            remote(
                gbuf.at[p, place], gbuf.at[p, place], g1_send.at[p * NO + q], g1_recv.at[p * NO + q], (p, c)
            ).wait_recv()
    gout_ref[...] = gbuf[...]
    gxout_ref[...] = gx[...]

    def spread_done():
        for q in col_peers:
            remote(gbuf.at[r, mine], gbuf.at[r, mine], g2_send.at[q], g2_recv.at[c], (r, q)).wait_send()

    owning(c, spread_done)
    for p in row_peers:
        for q in range(NO):
            place = pl.ds(q * CH2, CH2)
            remote(
                gbuf.at[r, place], gbuf.at[r, place], g1_send.at[p * NO + q], g1_recv.at[r * NO + q], (p, c)
            ).wait_send()
    for cp, cond in pending:
        if cond is None:
            cp.wait_send()
        else:
            pl.when(cond)(cp.wait_send)


def finish(cfg, pair_in, align_in, g_in, gx_in, pair_ref, align_ref, proj_ref, wg_ref, gg_ref, bg_ref):
    R, K, M, EX, CH1 = cfg
    pair_ref[...] = pair_in[...]
    align_ref[...] = align_in[...]
    for p in range(R):
        wg_ref[p * CH1:(p + 1) * CH1, :] = g_in[p].astype(F32)
    e = jnp.concatenate([gx_in[p].astype(F32) for p in range(M // EX)], axis=0)
    proj_ref[...] = e[:, :2 * K]
    flipped = jnp.transpose(e)
    gg_ref[...] = flipped[2 * K:2 * K + 1, :]
    bg_ref[...] = flipped[2 * K + 1:2 * K + 2, :]


def shards(x, gain, shift, mapping, w, bias, cot):
    R, C = lax.axis_size("row"), lax.axis_size("col")
    S, M = x.shape[0], x.shape[2]
    K = mapping.shape[1] // 2
    BR, BC, E = cot.shape
    rows = w.shape[0]
    CH1, EX = rows // R, max(16, M // R)
    CH2 = max(16, CH1 // C)
    NO = CH1 // CH2
    cfg = (R, C, BR, BC, S, M, K, CH1, EX, CH2, NO)
    vm = pl.BlockSpec(memory_space=pltpu.VMEM)
    hbm = pl.BlockSpec(memory_space=pltpu.HBM)
    sem = pltpu.SemaphoreType.DMA
    shape = jax.ShapeDtypeStruct
    params = pltpu.CompilerParams(
        collective_id=0, has_side_effects=True, vmem_limit_bytes=48 * 1024 * 1024
    )
    parts = pl.pallas_call(
        functools.partial(kernel, cfg),
        out_shape=[
            shape((BR * BC, E), BF16), shape((M, S), F32),
            shape((R, CH1, E), BF16), shape((R, EX, E), BF16),
        ],
        in_specs=[hbm] * 7,
        out_specs=[vm] * 4,
        scratch_shapes=[
            pltpu.VMEM((1, M), F32),
            pltpu.VMEM((1, M), F32),
            pltpu.VMEM(mapping.shape, BF16),
            pltpu.VMEM(w.shape, BF16),
            pltpu.VMEM((1, E), F32),
            pltpu.VMEM((BR * BC, E), BF16),
            pltpu.VMEM((BR + BC, M, S), BF16),
            pltpu.VMEM((K * BR, S), F32),
            pltpu.VMEM((BR * BC, E), F32),
            pltpu.VMEM((BR * BC, E), F32),
            pltpu.VMEM((K * BR, S), F32),
            pltpu.VMEM((BR, K, S), BF16),
            pltpu.VMEM((BC, K, S), BF16),
            pltpu.VMEM((C, K, S), BF16),
            pltpu.VMEM((R, K, S), BF16),
            pltpu.VMEM((R, CH1, E), BF16),
            pltpu.VMEM((R, CH1, E), BF16),
            pltpu.VMEM((CH1, E), BF16),
            pltpu.VMEM((C, CH2, E), BF16),
            pltpu.VMEM((R, CH1, E), BF16),
            pltpu.VMEM((M, E), F32),
            pltpu.VMEM((R, EX, E), BF16),
            pltpu.VMEM((R, EX, E), BF16),
            pltpu.VMEM((C, EX, E), BF16),
            pltpu.VMEM((R, EX, E), BF16),
            sem((7,)),
            sem((C + R,)), sem((BR + BC,)),
            sem((C + BC,)), sem((C + R,)),
            sem((R,)), sem((R,)),
            sem((C,)), sem((C,)),
            sem((C,)), sem((C,)),
            sem((R * NO,)), sem((R * NO,)),
            sem((R,)), sem((R,)),
            sem((C,)), sem((C,)),
            sem((R,)), sem((R,)),
        ],
        compiler_params=params,
        name="outer_mean",
    )(
        jnp.transpose(x, (1, 2, 0)).reshape(M, S), gain.reshape(1, M), shift.reshape(1, M), mapping, w,
        bias.reshape(1, E), cot.reshape(BR * BC, E),
    )
    pair, align, proj, wg, gg, bg = pl.pallas_call(
        functools.partial(finish, (R, K, M, EX, CH1)),
        out_shape=[
            shape((BR * BC, E), BF16), shape((M, S), F32), shape((M, 2 * K), F32),
            shape((rows, E), F32), shape((1, M), F32), shape((1, M), F32),
        ],
        in_specs=[vm] * 4,
        out_specs=[vm] * 6,
        compiler_params=pltpu.CompilerParams(vmem_limit_bytes=8 * 1024 * 1024),
        name="finish",
    )(*parts)
    return (
        pair.reshape(BR, BC, E), jnp.transpose(align.reshape(1, M, S), (2, 0, 1)), proj, wg,
        gg.reshape(M), bg.reshape(M),
    )


def solution(mesh):
    in_specs = (P(None, ("row", "col"), None), P(), P(), P(), P(), P(), P("row", "col", None))
    out_specs = (P("row", "col", None), P(None, ("row", "col"), None), P(), P(), P(), P())
    return jax.shard_map(shards, mesh=mesh, in_specs=in_specs, out_specs=out_specs, check_vma=False)
```

time: 39.9 us -> 37.4 us (0.937)
  local copies, waits for them, and re-layouts: 6.17 us -> 3.72 us
    unnamed x19 -> x14, local copies, waits for them, and re-layouts: 6.17 us -> 3.72 us
    pallas_call x1 -> x2, Pallas kernels: 32.7 us -> 32.6 us  [the longest x1 31.8 us: shards(): pl.pallas_call(functools.partial(kernel, cfg), out_shape=[shape((BR * BC,...]
where the time goes in v2:
time: 37.4 us; the launch traced here: 37 us
  Pallas kernels  32.6 us (87%)
  local copies, waits for them, and re-layouts  3.72 us (10%)
  between operations  0.67 us (2%)
    pallas_call x1, Pallas kernels, shards(): pl.pallas_call(functools.partial(kernel, cfg), out_shape=[shape((BR * BC,...  31.8 us
    unnamed x14, local copies, waits for them, and re-layouts  3.72 us
    pallas_call x1, Pallas kernels, shards(): pl.pallas_call(functools.partial(finish, (R, K, M, EX, CH1)), out_shape=[...  0.84 us

profile of v2, /device:TPU:0, one launch (start us, length us, event | category | flops | bytes accessed | tf_op | source)
XLA Modules:
  0.0 37.0 jit_solution(17781316537046656059)
XLA Ops:
  0.6 0.0 copy-start.3
  0.6 0.0 copy-start.4
  0.7 0.0 copy-start.5
  0.7 0.7 %copy-done.3 = bf16[8,4,128]{2,1,0:T(4,128)(2,1)S(1)} copy-done((bf16[8,4,128]{2,1,0:T(4,128)(2,1)S(1)}, bf16[8,4,128]{2,1,0:T(4,128)(2,1)}, u32[]{:S(2)}) %copy-start.3) | copy-done | bytes 8216
  1.3 0.0 copy-done.4
  1.3 0.0 copy-done.5
  1.3 0.0 copy-start
  1.3 0.9 %copy-done = bf16[1024,128]{1,0:T(8,128)(2,1)S(1)} copy-done((bf16[1024,128]{1,0:T(8,128)(2,1)S(1)}, bf16[1024,128]{1,0:T(8,128)(2,1)}, u32[]{:S(2)}) %copy-start) | copy-done | bytes 262168
  2.3 0.0 copy-start.1
  2.3 0.7 %copy-done.1 = bf16[128,1,64]{0,2,1:T(8,128)(2,1)S(1)} copy-done((bf16[128,1,64]{0,2,1:T(8,128)(2,1)S(1)}, bf16[128,1,64]{0,2,1:T(8,128)(2,1)}, u32[]{:S(2)}) %copy-start.1) | copy-done | bytes 16408
  3.0 0.0 copy-start.2
  3.0 0.7 %copy-done.2 = bf16[64,64]{1,0:T(8,128)(2,1)S(1)} copy-done((bf16[64,64]{1,0:T(8,128)(2,1)S(1)}, bf16[64,64]{1,0:T(8,128)(2,1)}, u32[]{:S(2)}) %copy-start.2) | copy-done | bytes 8216
  3.7 0.0 copy-start.6
  3.7 0.7 %copy-done.6 = f32[128]{0:T(128)S(1)} copy-done((f32[128]{0:T(128)S(1)}, f32[128]{0:T(128)}, u32[]{:S(2)}) %copy-start.6) | copy-done | bytes 536
  4.4 31.8 %outer_mean.1 = (bf16[32,128]{1,0:T(8,128)(2,1)S(1)}, f32[64,128]{1,0:T(8,128)S(1)}, bf16[4,256,128]{2,1,0:T(8,128)(2,1)S(1)}, bf16[4,16,128]{2,1,0:T(8,128)(2,1)S(1)}) custom-call(bf16[64,128]{1,0:T(8,128)(2,1)S(1)} %bitcast.13, f32[1,64]{1,0:T(1,128)S(1)} %bitcast.15, f32[1,64]{1,0:T(1,128)S(1)} %bitcast.16, bf16[64,64]{1,0:T(8,128)(2,1)S(1)} %copy-done.2, ...), custom_call_target="tpu_custom_call" | custom-call | tf_op jit(solution)/shard_map/outer_mean/pallas_call | solution.py:372
  36.2 0.8 %finish.1 = (bf16[32,128]{1,0:T(8,128)(2,1)}, f32[64,128]{1,0:T(8,128)}, f32[64,64]{1,0:T(8,128)}, f32[1024,128]{1,0:T(8,128)}, f32[1,64]{1,0:T(1,128)}, /*index=5*/f32[1,64]{1,0:T(1,128)}) custom-call(bf16[32,128]{1,0:T(8,128)(2,1)S(1)} %get-tuple-element.16.pair_in, f32[64,128]{1,0:T(8,128)S(1)} %get-tuple-element.17.align_in, ...), custom_call_target="tpu_custom_call" | custom-call | tf_op jit(solution)/shard_map/finish/pallas_call | solution.py:423
Async XLA Ops:
  0.6 0.7 %copy-start.3 = (bf16[8,4,128]{2,1,0:T(4,128)(2,1)S(1)}, bf16[8,4,128]{2,1,0:T(4,128)(2,1)}, u32[]{:S(2)}) copy-start(bf16[8,4,128]{2,1,0:T(4,128)(2,1)} %param.13) | copy-start | bytes 24580
  0.6 0.7 %copy-start.4 = (f32[64]{0:T(128)S(1)}, f32[64]{0:T(128)}, u32[]{:S(2)}) copy-start(f32[64]{0:T(128)} %param.8) | copy-start | bytes 772
  0.7 0.7 %copy-start.5 = (f32[64]{0:T(128)S(1)}, f32[64]{0:T(128)}, u32[]{:S(2)}) copy-start(f32[64]{0:T(128)} %param.9) | copy-start | bytes 772
  1.3 1.0 %copy-start = (bf16[1024,128]{1,0:T(8,128)(2,1)S(1)}, bf16[1024,128]{1,0:T(8,128)(2,1)}, u32[]{:S(2)}) copy-start(bf16[1024,128]{1,0:T(8,128)(2,1)} %w_hbm.1) | copy-start | bytes 786436
  2.3 0.7 %copy-start.1 = (bf16[128,1,64]{0,2,1:T(8,128)(2,1)S(1)}, bf16[128,1,64]{0,2,1:T(8,128)(2,1)}, u32[]{:S(2)}) copy-start(bf16[128,1,64]{0,2,1:T(8,128)(2,1)} %param.7) | copy-start | bytes 49156
  3.0 0.7 %copy-start.2 = (bf16[64,64]{1,0:T(8,128)(2,1)S(1)}, bf16[64,64]{1,0:T(8,128)(2,1)}, u32[]{:S(2)}) copy-start(bf16[64,64]{1,0:T(8,128)(2,1)} %map_hbm.1) | copy-start | bytes 24580
  3.7 0.7 %copy-start.6 = (f32[128]{0:T(128)S(1)}, f32[128]{0:T(128)}, u32[]{:S(2)}) copy-start(f32[128]{0:T(128)} %param.12) | copy-start | bytes 1540

commit v3 on v2

--- a/solution.py
+++ b/solution.py
@@ -37,7 +37,7 @@
     cfg, x_hbm, gain_hbm, shift_hbm, map_hbm, w_hbm, bias_hbm, cot_hbm,
     pair_ref, align_ref, gout_ref, gxout_ref,
     gain_ref, shift_ref, map_ref, w_ref, bias_ref, cot_ref,
-    xbuf, lf, cotf, pairf, glf, sl, sr, rl, rr, s1, r1, s2, r2, gbuf, ebuf, s1x, r1x, r2x, gx,
+    xown, lbuf, rbuf, lf, cotf, pairf, glf, sl, sr, rl, rr, s1, r1, s2, r2, gbuf, ebuf, s1x, r1x, r2x, gx, pr,
     load, x_send, x_recv, e_send, e_recv, s1_send, s1_recv, s2_send, s2_recv,
     g2_send, g2_recv, g1_send, g1_recv, x1_send, x1_recv, x2_send, x2_recv, x3_send, x3_recv,
 ):
@@ -53,7 +53,7 @@
     loads = [
         pltpu.make_async_copy(src, dst, load.at[i])
         for i, (src, dst) in enumerate([
-            (x_hbm, xbuf.at[c]), (cot_hbm, cot_ref), (w_hbm, w_ref), (map_hbm, map_ref),
+            (x_hbm, xown), (cot_hbm, cot_ref), (w_hbm, w_ref), (map_hbm, map_ref),
             (gain_hbm, gain_ref), (shift_hbm, shift_ref), (bias_hbm, bias_ref),
         ])
     ]
@@ -96,11 +96,28 @@
         def _():
             signal(owners[k])
 
-    loads[0].wait()
+    def standardized(x):
+        mean = jnp.mean(x, axis=0, keepdims=True)
+        cen = x - mean
+        scale = lax.rsqrt(jnp.mean(cen * cen, axis=0, keepdims=True) + 1e-05)
+        return cen * scale, scale
+
+    early = (0, 3, 4, 5)
+    for i in early:
+        loads[i].wait()
+    factor = jnp.transpose(jnp.broadcast_to(gain_ref[...], (S, M)))
+    shift = jnp.transpose(jnp.broadcast_to(shift_ref[...], (S, M)))
+    mapping = map_ref[...]
+    mapping_t = jnp.transpose(mapping.astype(F32)).astype(BF16)
+    own_unit, own_scale = standardized(xown[...].astype(F32))
+    normed = (own_unit * factor + shift).astype(BF16)
+    proj = dot(mapping_t, normed, 1, 0).astype(BF16)
+    lbuf[c] = proj[:K]
+    pr[...] = proj[K:]
 
     @pl.when(self_right)
     def _():
-        xbuf[BR + dest_slot] = xbuf[c]
+        rbuf[dest_slot] = proj[K:]
 
     pl.semaphore_wait(barrier, C - 1 + R - 1 + R + BC - jnp.where(self_right, 2, 0))
 
@@ -116,18 +133,15 @@
 
     for q in range(R):
         send(
-            xbuf.at[c], xbuf.at[BR + dest_slot], x_send.at[C + q], x_recv.at[BR + dest_slot],
+            pr, rbuf.at[dest_slot], x_send.at[C + q], x_recv.at[BR + dest_slot],
             (q, dest_col), other(q, dest_col),
         )
     for q in col_peers:
-        send(xbuf.at[c], xbuf.at[c], x_send.at[q], x_recv.at[c], (r, q))
-
-    for cp in loads[1:]:
-        cp.wait()
-    factor = jnp.transpose(jnp.broadcast_to(gain_ref[...], (S, M)))
-    shift = jnp.transpose(jnp.broadcast_to(shift_ref[...], (S, M)))
-    mapping = map_ref[...]
-    mapping_t = jnp.transpose(mapping.astype(F32)).astype(BF16)
+        send(lbuf.at[c], lbuf.at[c], x_send.at[q], x_recv.at[c], (r, q))
+
+    for i in range(len(loads)):
+        if i not in early:
+            loads[i].wait()
     cotf[...] = cot_ref[...].astype(F32)
     cot = jnp.concatenate([cotf[pl.ds(j, BR, stride=BC), :] for j in range(BC)], axis=0).astype(BF16)
     w = w_ref[...]
@@ -143,36 +157,19 @@
         tiles.append(jnp.stack(b, axis=1).reshape(K * BR, 128))
     g2 = jnp.concatenate(tiles, axis=1).astype(BF16)
 
-    def standardized(x):
-        mean = jnp.mean(x, axis=0, keepdims=True)
-        cen = x - mean
-        scale = lax.rsqrt(jnp.mean(cen * cen, axis=0, keepdims=True) + 1e-05)
-        return cen * scale, scale
-
-    own_unit, own_scale = standardized(xbuf[c].astype(F32))
-
-    for q in col_peers:
-        remote(xbuf.at[q], xbuf.at[q], x_send.at[q], x_recv.at[q], (r, q)).wait_recv()
+    for q in col_peers:
+        remote(lbuf.at[q], lbuf.at[q], x_send.at[q], x_recv.at[q], (r, q)).wait_recv()
     for k in range(BC):
         @pl.when(other(*owners[k]))
         def _():
             remote(
-                xbuf.at[BR + k], xbuf.at[BR + k], x_send.at[0], x_recv.at[BR + k], owners[k]
+                rbuf.at[k], rbuf.at[k], x_send.at[0], x_recv.at[BR + k], owners[k]
             ).wait_recv()
 
-    units, normeds = [], []
-    for i in range(BR + BC):
-        unit, _ = standardized(xbuf[i].astype(F32))
-        units.append(unit)
-        normeds.append((unit * factor + shift).astype(BF16))
-    normed = jnp.concatenate(normeds, axis=1)
-    proj = dot(mapping_t, normed, 1, 0)
     for i in range(BR):
-        lf[pl.ds(i, K, stride=BR), :] = proj[:K, S * i:S * i + S].astype(BF16).astype(F32)
+        lf[pl.ds(i, K, stride=BR), :] = lbuf[i].astype(F32)
     left = lf[...].astype(BF16)
-    right = jnp.concatenate(
-        [proj[K:, S * (BR + j):S * (BR + j) + S] for j in range(BC)], axis=0
-    ).astype(BF16)
+    right = jnp.concatenate([rbuf[j] for j in range(BC)], axis=0)
     outer = (dot(left, right, 1, 1) * inv).astype(BF16).astype(F32)
     rows = []
     for t in range(BC // 4):
@@ -190,15 +187,11 @@
 
     glf[...] = dot(g2, right, 1, 0) * inv
     gr = (dot(g2, left, 0, 0) * inv).astype(BF16)
-    gls = []
     for i in range(BR):
         gl = glf[pl.ds(i, K, stride=BR), :].astype(BF16)
-        gls.append(gl)
         sl[i] = gl
-    grs = []
     for j in range(BC):
         gg = gr[j * K:(j + 1) * K]
-        grs.append(gg)
         sr[j] = gg
     rl[c] = sl[c]
 
@@ -211,20 +204,36 @@
     for k in range(BC):
         send(sr.at[k], rr.at[r], e_send.at[C + k], e_recv.at[C + r], owners[k], other(*owners[k]))
 
-    glc = jnp.concatenate(gls, axis=1)
-    grc = jnp.concatenate(grs, axis=1)
-    cut = BR * S
+    def total(buf, count):
+        acc = buf[0].astype(F32)
+        for p in range(1, count):
+            acc = acc + buf[p].astype(F32)
+        return acc
+
+    r1[r] = s1[r]
+    for p in row_peers:
+        remote(s1.at[p], r1.at[p], s1_send.at[p], s1_recv.at[p], (p, c)).wait_recv()
+    s2[...] = total(r1, R).astype(BF16)
+
+    def chunk(q):
+        return pl.ds(pl.multiple_of(lax.rem(q, NO) * CH2, 16), CH2)
+
+    for q in col_peers:
+        send(s2.at[chunk(q)], r2.at[c], s2_send.at[q], s2_recv.at[c], (r, q))
+    r2[c] = s2[chunk(c)]
+
+    for q in col_peers:
+        remote(sl.at[q], rl.at[q], e_send.at[q], e_recv.at[q], (r, q)).wait_recv()
+    for q in range(R):
+        @pl.when(other(q, dest_col))
+        def _():
+            remote(sr.at[0], rr.at[q], e_send.at[C], e_recv.at[C + q], (q, dest_col)).wait_recv()
+    act = jnp.concatenate([total(rl, C), total(rr, R)], axis=0).astype(BF16)
+    grad_normed = dot(mapping, act, 1, 0)
     ebuf[...] = jnp.zeros_like(ebuf)
-    ebuf[:, :K] = dot(normed[:, :cut], glc, 1, 1)
-    ebuf[:, K:2 * K] = dot(normed[:, cut:], grc, 1, 1)
-    gn = jnp.concatenate([dot(mapping[:, :K], glc, 1, 0), dot(mapping[:, K:], grc, 1, 0)], axis=1)
-    bsum, gsum = jnp.zeros((M, S), F32), jnp.zeros((M, S), F32)
-    for i in range(BR + BC):
-        piece = gn[:, S * i:S * i + S]
-        bsum = bsum + piece
-        gsum = gsum + piece * units[i]
-    ebuf[:, 2 * K:2 * K + 1] = jnp.sum(gsum, axis=1, keepdims=True)
-    ebuf[:, 2 * K + 1:2 * K + 2] = jnp.sum(bsum, axis=1, keepdims=True)
+    ebuf[:, :2 * K] = dot(normed, act, 1, 1)
+    ebuf[:, 2 * K:2 * K + 1] = jnp.sum(grad_normed * own_unit, axis=1, keepdims=True)
+    ebuf[:, 2 * K + 1:2 * K + 2] = jnp.sum(grad_normed, axis=1, keepdims=True)
     extra = ebuf[...].astype(BF16)
     for p in range(R):
         if p * EX < M:
@@ -233,36 +242,24 @@
             s1x[p] = jnp.zeros((EX, 128), BF16)
     for p in row_peers:
         send(s1x.at[p], r1x.at[r], x1_send.at[p], x1_recv.at[r], (p, c))
-
-    def total(buf, count):
-        acc = buf[0].astype(F32)
-        for p in range(1, count):
-            acc = acc + buf[p].astype(F32)
-        return acc
-
-    r1[r] = s1[r]
-    for p in row_peers:
-        remote(s1.at[p], r1.at[p], s1_send.at[p], s1_recv.at[p], (p, c)).wait_recv()
-    s2[...] = total(r1, R).astype(BF16)
-
-    def chunk(q):
-        return pl.ds(pl.multiple_of(lax.rem(q, NO) * CH2, 16), CH2)
-
-    for q in col_peers:
-        send(s2.at[chunk(q)], r2.at[c], s2_send.at[q], s2_recv.at[c], (r, q))
-    r2[c] = s2[chunk(c)]
-
-    r1x[r] = s1x[r]
-    for p in row_peers:
-        remote(s1x.at[p], r1x.at[p], x1_send.at[p], x1_recv.at[p], (p, c)).wait_recv()
-    r2x[c] = total(r1x, R).astype(BF16)
-    for q in col_peers:
-        send(r2x.at[c], r2x.at[c], x2_send.at[q], x2_recv.at[c], (r, q))
+    scaled = grad_normed * factor
+    align_ref[...] = own_scale * (
+        scaled
+        - jnp.mean(scaled, axis=0, keepdims=True)
+        - own_unit * jnp.mean(scaled * own_unit, axis=0, keepdims=True)
+    )
 
     pairs = dot(ot, w, 1, 0) + bias_ref[...]
     for j in range(BC):
         pairf[pl.ds(j, BR, stride=BC), :] = pairs[j * BR:(j + 1) * BR]
     pair_ref[...] = pairf[...].astype(BF16)
+
+    r1x[r] = s1x[r]
+    for p in row_peers:
+        remote(s1x.at[p], r1x.at[p], x1_send.at[p], x1_recv.at[p], (p, c)).wait_recv()
+    r2x[c] = total(r1x, R).astype(BF16)
+    for q in col_peers:
+        send(r2x.at[c], r2x.at[c], x2_send.at[q], x2_recv.at[c], (r, q))
 
     for q in col_peers:
         remote(s2.at[chunk(q)], r2.at[q], s2_send.at[q], s2_recv.at[q], (r, q)).wait_recv()
@@ -290,20 +287,6 @@
     gx[r] = total(r2x, C).astype(BF16)
     for p in row_peers:
         send(gx.at[r], gx.at[r], x3_send.at[p], x3_recv.at[r], (p, c))
-
-    for q in col_peers:
-        remote(sl.at[q], rl.at[q], e_send.at[q], e_recv.at[q], (r, q)).wait_recv()
-    for q in range(R):
-        @pl.when(other(q, dest_col))
-        def _():
-            remote(sr.at[0], rr.at[q], e_send.at[C], e_recv.at[C + q], (q, dest_col)).wait_recv()
-    act = jnp.concatenate([total(rl, C), total(rr, R)], axis=0).astype(BF16)
-    scaled = dot(mapping, act, 1, 0) * factor
-    align_ref[...] = own_scale * (
-        scaled
-        - jnp.mean(scaled, axis=0, keepdims=True)
-        - own_unit * jnp.mean(scaled * own_unit, axis=0, keepdims=True)
-    )
 
     for q in col_peers:
         def pass_on():
@@ -367,7 +350,7 @@
     sem = pltpu.SemaphoreType.DMA
     shape = jax.ShapeDtypeStruct
     params = pltpu.CompilerParams(
-        collective_id=0, has_side_effects=True, vmem_limit_bytes=48 * 1024 * 1024
+        collective_id=0, has_side_effects=True, vmem_limit_bytes=58 * 1024 * 1024
     )
     parts = pl.pallas_call(
         functools.partial(kernel, cfg),
@@ -384,7 +367,9 @@
             pltpu.VMEM(w.shape, BF16),
             pltpu.VMEM((1, E), F32),
             pltpu.VMEM((BR * BC, E), BF16),
-            pltpu.VMEM((BR + BC, M, S), BF16),
+            pltpu.VMEM((M, S), BF16),
+            pltpu.VMEM((BR, K, S), BF16),
+            pltpu.VMEM((BC, K, S), BF16),
             pltpu.VMEM((K * BR, S), F32),
             pltpu.VMEM((BR * BC, E), F32),
             pltpu.VMEM((BR * BC, E), F32),
@@ -403,6 +388,7 @@
             pltpu.VMEM((R, EX, E), BF16),
             pltpu.VMEM((C, EX, E), BF16),
             pltpu.VMEM((R, EX, E), BF16),
+            pltpu.VMEM((K, S), BF16),
             sem((7,)),
             sem((C + R,)), sem((BR + BC,)),
             sem((C + BC,)), sem((C + R,)),
@@ -428,7 +414,7 @@
         ],
         in_specs=[vm] * 4,
         out_specs=[vm] * 6,
-        compiler_params=pltpu.CompilerParams(vmem_limit_bytes=8 * 1024 * 1024),
+        compiler_params=pltpu.CompilerParams(vmem_limit_bytes=58 * 1024 * 1024),
         name="finish",
     )(*parts)
     return (

time: 37.4 us -> 32.9 us (0.88)
  local copies, waits for them, and re-layouts: 3.72 us -> 0 us
  Pallas kernels: 32.6 us -> 32 us
    unnamed x14 -> x0, local copies, waits for them, and re-layouts: 3.72 us -> none
    pallas_call x1, Pallas kernels: 31.8 us -> 30.2 us  [shards(): pl.pallas_call(functools.partial(kernel, cfg), out_shape=[shape((BR * BC,...]
    pallas_call x1, Pallas kernels: 0.84 us -> 1.83 us  [shards(): pl.pallas_call(functools.partial(finish, (R, K, M, EX, CH1)), out_shape=[...]
where the time goes in v3:
time: 32.9 us; the launch traced here: 32.7 us
  Pallas kernels  32 us (97%)
  between operations  0.64 us (2%)
    pallas_call x1, Pallas kernels, shards(): pl.pallas_call(functools.partial(kernel, cfg), out_shape=[shape((BR * BC,...  30.2 us
    pallas_call x1, Pallas kernels, shards(): pl.pallas_call(functools.partial(finish, (R, K, M, EX, CH1)), out_shape=[...  1.83 us

profile of v3, /device:TPU:0, one launch (start us, length us, event | category | flops | bytes accessed | tf_op | source)
XLA Modules:
  0.0 32.7 jit_solution(15688216580757505930)
XLA Ops:
  0.6 30.2 %outer_mean.1 = (bf16[32,128]{1,0:T(8,128)(2,1)}, f32[64,128]{1,0:T(8,128)}, bf16[4,256,128]{2,1,0:T(8,128)(2,1)}, bf16[4,16,128]{2,1,0:T(8,128)(2,1)}) custom-call(bf16[64,128]{1,0:T(8,128)(2,1)} %bitcast.13, f32[1,64]{1,0:T(1,128)} %bitcast.15, f32[1,64]{1,0:T(1,128)} %bitcast.16, bf16[64,64]{1,0:T(8,128)(2,1)} %map_hbm.1, bf16[1024,128]{1,0:T(8,128)(2,1)} %w_hbm.1, ...), custom_call_target="tpu_custom_call" | custom-call | tf_op jit(solution)/shard_map/outer_mean/pallas_call | solution.py:355
  30.8 1.8 %finish.1 = (bf16[32,128]{1,0:T(8,128)(2,1)}, f32[64,128]{1,0:T(8,128)}, f32[64,64]{1,0:T(8,128)}, f32[1024,128]{1,0:T(8,128)}, f32[1,64]{1,0:T(1,128)}, /*index=5*/f32[1,64]{1,0:T(1,128)}) custom-call(bf16[32,128]{1,0:T(8,128)(2,1)} %get-tuple-element.16.pair_in, f32[64,128]{1,0:T(8,128)} %get-tuple-element.17.align_in, ...), custom_call_target="tpu_custom_call" | custom-call | tf_op jit(solution)/shard_map/finish/pallas_call | solution.py:409

commit v4 on v3

--- a/solution.py
+++ b/solution.py
@@ -37,7 +37,7 @@
     cfg, x_hbm, gain_hbm, shift_hbm, map_hbm, w_hbm, bias_hbm, cot_hbm,
     pair_ref, align_ref, gout_ref, gxout_ref,
     gain_ref, shift_ref, map_ref, w_ref, bias_ref, cot_ref,
-    xown, lbuf, rbuf, lf, cotf, pairf, glf, sl, sr, rl, rr, s1, r1, s2, r2, gbuf, ebuf, s1x, r1x, r2x, gx, pr,
+    xown, lbuf, rbuf, lf, cotf, pairf, glf, sl, sr, rl, rr, s1, r1, s2, r2, gbuf, ebuf, s1x, r1x, r2x, gx, pr, alignf, pairb, store,
     load, x_send, x_recv, e_send, e_recv, s1_send, s1_recv, s2_send, s2_recv,
     g2_send, g2_recv, g1_send, g1_recv, x1_send, x1_recv, x2_send, x2_recv, x3_send, x3_recv,
 ):
@@ -243,16 +243,20 @@
     for p in row_peers:
         send(s1x.at[p], r1x.at[r], x1_send.at[p], x1_recv.at[r], (p, c))
     scaled = grad_normed * factor
-    align_ref[...] = own_scale * (
+    alignf[...] = own_scale * (
         scaled
         - jnp.mean(scaled, axis=0, keepdims=True)
         - own_unit * jnp.mean(scaled * own_unit, axis=0, keepdims=True)
     )
 
+    stores = [pltpu.make_async_copy(alignf, align_ref, store.at[0])]
+    stores[0].start()
     pairs = dot(ot, w, 1, 0) + bias_ref[...]
     for j in range(BC):
         pairf[pl.ds(j, BR, stride=BC), :] = pairs[j * BR:(j + 1) * BR]
-    pair_ref[...] = pairf[...].astype(BF16)
+    pairb[...] = pairf[...].astype(BF16)
+    stores.append(pltpu.make_async_copy(pairb, pair_ref, store.at[1]))
+    stores[1].start()
 
     r1x[r] = s1x[r]
     for p in row_peers:
@@ -267,18 +271,21 @@
     mine = chunk(c)
     result = total(r2, C).astype(BF16)
 
-    def forward(q):
-        place = chunk(q)
-        for p in row_peers:
-            remote(
-                gbuf.at[r, place], gbuf.at[r, place], g1_send.at[p * NO + q], g1_recv.at[r * NO + q], (p, c)
-            ).start()
+    half = NO // 2
+    near = lax.div(lax.rem(c, NO), half)
+
+    def group(h):
+        return pl.ds(pl.multiple_of(h * half * CH2, 16), half * CH2)
+
+    def forward(h, p):
+        return remote(
+            gbuf.at[r, group(h)], gout_ref.at[r, group(h)], g1_send.at[p * 2 + h], g1_recv.at[r * 2 + h], (p, c)
+        )
 
     def spread():
         gbuf[r, mine, :] = result
         for q in col_peers:
             remote(gbuf.at[r, mine], gbuf.at[r, mine], g2_send.at[q], g2_recv.at[c], (r, q)).start()
-        forward(c)
 
     owning(c, spread)
 
@@ -286,23 +293,30 @@
         remote(r2x.at[q], r2x.at[q], x2_send.at[q], x2_recv.at[q], (r, q)).wait_recv()
     gx[r] = total(r2x, C).astype(BF16)
     for p in row_peers:
-        send(gx.at[r], gx.at[r], x3_send.at[p], x3_recv.at[r], (p, c))
-
-    for q in col_peers:
-        def pass_on():
-            place = chunk(q)
-            remote(gbuf.at[r, place], gbuf.at[r, place], g2_send.at[q], g2_recv.at[q], (r, q)).wait_recv()
-            forward(q)
-        owning(q, pass_on)
-    for p in row_peers:
-        remote(gx.at[p], gx.at[p], x3_send.at[p], x3_recv.at[p], (p, c)).wait_recv()
-        for q in range(NO):
-            place = pl.ds(q * CH2, CH2)
+        send(gx.at[r], gxout_ref.at[r], x3_send.at[p], x3_recv.at[r], (p, c))
+    stores.append(pltpu.make_async_copy(gx.at[r], gxout_ref.at[r], store.at[3]))
+    stores[-1].start()
+
+    for h in (near, 1 - near):
+        for t in range(half):
+            q = h * half + t
+
+            @pl.when(q != c)
+            def _():
+                place = chunk(q)
+                remote(gbuf.at[r, place], gbuf.at[r, place], g2_send.at[q], g2_recv.at[q], (r, q)).wait_recv()
+        for p in row_peers:
+            forward(h, p).start()
+    stores.append(pltpu.make_async_copy(gbuf.at[r], gout_ref.at[r], store.at[2]))
+    stores[-1].start()
+    for p in row_peers:
+        remote(gx.at[p], gxout_ref.at[p], x3_send.at[p], x3_recv.at[p], (p, c)).wait_recv()
+        for h in range(2):
             remote(
-                gbuf.at[p, place], gbuf.at[p, place], g1_send.at[p * NO + q], g1_recv.at[p * NO + q], (p, c)
+                gbuf.at[p, group(h)], gout_ref.at[p, group(h)], g1_send.at[p * 2 + h], g1_recv.at[p * 2 + h], (p, c)
             ).wait_recv()
-    gout_ref[...] = gbuf[...]
-    gxout_ref[...] = gx[...]
+    for cp in stores:
+        cp.wait()
 
     def spread_done():
         for q in col_peers:
@@ -310,11 +324,8 @@
 
     owning(c, spread_done)
     for p in row_peers:
-        for q in range(NO):
-            place = pl.ds(q * CH2, CH2)
-            remote(
-                gbuf.at[r, place], gbuf.at[r, place], g1_send.at[p * NO + q], g1_recv.at[r * NO + q], (p, c)
-            ).wait_send()
+        for h in range(2):
+            forward(h, p).wait_send()
     for cp, cond in pending:
         if cond is None:
             cp.wait_send()
@@ -359,7 +370,7 @@
             shape((R, CH1, E), BF16), shape((R, EX, E), BF16),
         ],
         in_specs=[hbm] * 7,
-        out_specs=[vm] * 4,
+        out_specs=[hbm] * 4,
         scratch_shapes=[
             pltpu.VMEM((1, M), F32),
             pltpu.VMEM((1, M), F32),
@@ -389,13 +400,16 @@
             pltpu.VMEM((C, EX, E), BF16),
             pltpu.VMEM((R, EX, E), BF16),
             pltpu.VMEM((K, S), BF16),
+            pltpu.VMEM((M, S), F32),
+            pltpu.VMEM((BR * BC, E), BF16),
+            sem((4,)),
             sem((7,)),
             sem((C + R,)), sem((BR + BC,)),
             sem((C + BC,)), sem((C + R,)),
             sem((R,)), sem((R,)),
             sem((C,)), sem((C,)),
             sem((C,)), sem((C,)),
-            sem((R * NO,)), sem((R * NO,)),
+            sem((R * 2,)), sem((R * 2,)),
             sem((R,)), sem((R,)),
             sem((C,)), sem((C,)),
             sem((R,)), sem((R,)),

time: 32.9 us -> 32.1 us (0.976)
  Pallas kernels: 32 us -> 31.2 us
    pallas_call x1, Pallas kernels: 30.2 us -> 29.4 us  [shards(): pl.pallas_call(functools.partial(kernel, cfg), out_shape=[shape((BR * BC,...]
where the time goes in v4:
time: 32.1 us; the launch traced here: 31.9 us
  Pallas kernels  31.2 us (97%)
  between operations  0.64 us (2%)
    pallas_call x1, Pallas kernels, shards(): pl.pallas_call(functools.partial(kernel, cfg), out_shape=[shape((BR * BC,...  29.4 us
    pallas_call x1, Pallas kernels, shards(): pl.pallas_call(functools.partial(finish, (R, K, M, EX, CH1)), out_shape=[...  1.83 us

profile of v4, /device:TPU:0, one launch (start us, length us, event | category | flops | bytes accessed | tf_op | source)
XLA Modules:
  0.0 31.9 jit_solution(7296152314150692476)
XLA Ops:
  0.6 29.4 %outer_mean.1 = (bf16[32,128]{1,0:T(8,128)(2,1)}, f32[64,128]{1,0:T(8,128)}, bf16[4,256,128]{2,1,0:T(8,128)(2,1)}, bf16[4,16,128]{2,1,0:T(8,128)(2,1)}) custom-call(bf16[64,128]{1,0:T(8,128)(2,1)} %bitcast.13, f32[1,64]{1,0:T(1,128)} %bitcast.15, f32[1,64]{1,0:T(1,128)} %bitcast.16, bf16[64,64]{1,0:T(8,128)(2,1)} %map_hbm.1, bf16[1024,128]{1,0:T(8,128)(2,1)} %w_hbm.1, ...), custom_call_target="tpu_custom_call" | custom-call | tf_op jit(solution)/shard_map/outer_mean/pallas_call | solution.py:366
  30.0 1.8 %finish.1 = (bf16[32,128]{1,0:T(8,128)(2,1)}, f32[64,128]{1,0:T(8,128)}, f32[64,64]{1,0:T(8,128)}, f32[1024,128]{1,0:T(8,128)}, f32[1,64]{1,0:T(1,128)}, /*index=5*/f32[1,64]{1,0:T(1,128)}) custom-call(bf16[32,128]{1,0:T(8,128)(2,1)} %get-tuple-element.16.pair_in, f32[64,128]{1,0:T(8,128)} %get-tuple-element.17.align_in, ...), custom_call_target="tpu_custom_call" | custom-call | tf_op jit(solution)/shard_map/finish/pallas_call | solution.py:423

commit v5 on v4

--- a/solution.py
+++ b/solution.py
@@ -131,13 +131,13 @@
             pl.when(cond)(cp.start)
         pending.append((cp, cond))
 
+    for q in col_peers:
+        send(lbuf.at[c], lbuf.at[c], x_send.at[q], x_recv.at[c], (r, q))
     for q in range(R):
         send(
             pr, rbuf.at[dest_slot], x_send.at[C + q], x_recv.at[BR + dest_slot],
             (q, dest_col), other(q, dest_col),
         )
-    for q in col_peers:
-        send(lbuf.at[c], lbuf.at[c], x_send.at[q], x_recv.at[c], (r, q))
 
     for i in range(len(loads)):
         if i not in early:
@@ -210,6 +210,14 @@
             acc = acc + buf[p].astype(F32)
         return acc
 
+    stores = []
+    pairs = dot(ot, w, 1, 0) + bias_ref[...]
+    for j in range(BC):
+        pairf[pl.ds(j, BR, stride=BC), :] = pairs[j * BR:(j + 1) * BR]
+    pairb[...] = pairf[...].astype(BF16)
+    stores.append(pltpu.make_async_copy(pairb, pair_ref, store.at[1]))
+    stores[-1].start()
+
     r1[r] = s1[r]
     for p in row_peers:
         remote(s1.at[p], r1.at[p], s1_send.at[p], s1_recv.at[p], (p, c)).wait_recv()
@@ -249,15 +257,8 @@
         - own_unit * jnp.mean(scaled * own_unit, axis=0, keepdims=True)
     )
 
-    stores = [pltpu.make_async_copy(alignf, align_ref, store.at[0])]
-    stores[0].start()
-    pairs = dot(ot, w, 1, 0) + bias_ref[...]
-    for j in range(BC):
-        pairf[pl.ds(j, BR, stride=BC), :] = pairs[j * BR:(j + 1) * BR]
-    pairb[...] = pairf[...].astype(BF16)
-    stores.append(pltpu.make_async_copy(pairb, pair_ref, store.at[1]))
-    stores[1].start()
-
+    stores.append(pltpu.make_async_copy(alignf, align_ref, store.at[0]))
+    stores[-1].start()
     r1x[r] = s1x[r]
     for p in row_peers:
         remote(s1x.at[p], r1x.at[p], x1_send.at[p], x1_recv.at[p], (p, c)).wait_recv()

time: 32.1 us -> 32 us (level)
  no operation moved by 1% of the time
where the time goes in v5:
time: 32 us; the launch traced here: 31.7 us
  Pallas kernels  31.1 us (97%)
  between operations  0.64 us (2%)
    pallas_call x1, Pallas kernels, shards(): pl.pallas_call(functools.partial(kernel, cfg), out_shape=[shape((BR * BC,...  29.2 us
    pallas_call x1, Pallas kernels, shards(): pl.pallas_call(functools.partial(finish, (R, K, M, EX, CH1)), out_shape=[...  1.83 us

profile of v5, /device:TPU:0, one launch (start us, length us, event | category | flops | bytes accessed | tf_op | source)
XLA Modules:
  0.0 31.7 jit_solution(14057126152717073474)
XLA Ops:
  0.6 29.2 %outer_mean.1 = (bf16[32,128]{1,0:T(8,128)(2,1)}, f32[64,128]{1,0:T(8,128)}, bf16[4,256,128]{2,1,0:T(8,128)(2,1)}, bf16[4,16,128]{2,1,0:T(8,128)(2,1)}) custom-call(bf16[64,128]{1,0:T(8,128)(2,1)} %bitcast.13, f32[1,64]{1,0:T(1,128)} %bitcast.15, f32[1,64]{1,0:T(1,128)} %bitcast.16, bf16[64,64]{1,0:T(8,128)(2,1)} %map_hbm.1, bf16[1024,128]{1,0:T(8,128)(2,1)} %w_hbm.1, ...), custom_call_target="tpu_custom_call" | custom-call | tf_op jit(solution)/shard_map/outer_mean/pallas_call | solution.py:367
  29.9 1.8 %finish.1 = (bf16[32,128]{1,0:T(8,128)(2,1)}, f32[64,128]{1,0:T(8,128)}, f32[64,64]{1,0:T(8,128)}, f32[1024,128]{1,0:T(8,128)}, f32[1,64]{1,0:T(1,128)}, /*index=5*/f32[1,64]{1,0:T(1,128)}) custom-call(bf16[32,128]{1,0:T(8,128)(2,1)} %get-tuple-element.16.pair_in, f32[64,128]{1,0:T(8,128)} %get-tuple-element.17.align_in, ...), custom_call_target="tpu_custom_call" | custom-call | tf_op jit(solution)/shard_map/finish/pallas_call | solution.py:424
